TPU v7x, 32 devices: a whole 2x2x4 slice. The times are simulated.
32 devices in a mesh: dp: 4 (over x, core), fsdp: 8 (over z, y).
Axes of the slice: x: 2, y: 2, z: 4, core: 2. Of those that a mesh axis runs over, the one named last changes fastest.
Arguments:
- frames: bfloat16 [51200, 640], P(('dp', 'fsdp')), may hold values from -6 to 6
- cotangent: bfloat16 [51200, 640], P(('dp', 'fsdp')), may hold values from -6 to 6
- span_starts: int32 [128, 32], P(('dp', 'fsdp')), may hold values from 0 to 390
- query_weight: bfloat16 [768, 768], P('fsdp'), may hold values from -0.25 to 0.25
- key_weight: bfloat16 [768, 768], P('fsdp'), may hold values from -0.25 to 0.25
- value_weight: bfloat16 [768, 768], P('fsdp'), may hold values from -0.25 to 0.25
- out_weight: bfloat16 [768, 768], P('fsdp'), may hold values from -3 to 3
- query_bias: bfloat16 [768], P('fsdp'), may hold values from -2.390625 to 2.390625
- value_bias: bfloat16 [768], P('fsdp'), may hold values from -2.390625 to 2.390625
- out_bias: bfloat16 [768], P('fsdp'), may hold values from -2.390625 to 2.390625
- first_gain: bfloat16 [768], P('fsdp'), may hold values from 0.3984375 to 1.59375
- first_shift: bfloat16 [768], P('fsdp'), may hold values from -2.390625 to 2.390625
- up_weight: bfloat16 [768, 3072], P('fsdp'), may hold values from -0.25 to 0.25
- up_bias: bfloat16 [3072], P('fsdp'), may hold values from -2.390625 to 2.390625
- down_weight: bfloat16 [3072, 768], P('fsdp'), may hold values from -0.15625 to 0.15625
- down_bias: bfloat16 [768], P('fsdp'), may hold values from -2.390625 to 2.390625
- second_gain: bfloat16 [768], P('fsdp'), may hold values from 0.3984375 to 1.59375
- second_shift: bfloat16 [768], P('fsdp'), may hold values from -2.390625 to 2.390625
- mask_vector: bfloat16 [768], P('fsdp'), may hold values from -5 to 5
Outputs:
- output: bfloat16 [51200, 640], P(('dp', 'fsdp'))
- frames_grad: bfloat16 [51200, 640], P(('dp', 'fsdp'))
- query_weight_grad: float32 [768, 768], P('fsdp')
- key_weight_grad: float32 [768, 768], P('fsdp')
- value_weight_grad: float32 [768, 768], P('fsdp')
- out_weight_grad: float32 [768, 768], P('fsdp')
- query_bias_grad: float32 [768], P('fsdp')
- value_bias_grad: float32 [768], P('fsdp')
- out_bias_grad: float32 [768], P('fsdp')
- first_gain_grad: float32 [768], P('fsdp')
- first_shift_grad: float32 [768], P('fsdp')
- up_weight_grad: float32 [768, 3072], P('fsdp')
- up_bias_grad: float32 [3072], P('fsdp')
- down_weight_grad: float32 [3072, 768], P('fsdp')
- down_bias_grad: float32 [768], P('fsdp')
- second_gain_grad: float32 [768], P('fsdp')
- second_shift_grad: float32 [768], P('fsdp')
- mask_vector_grad: float32 [768], P('fsdp')
Inputs may be any that keep to these rules, and one draw needn't show every extreme that they name: `span_starts`: first frame of a masked span of 10 frames within its utterance; spans may intersect.
All inputs are finite; a program needn't handle non-finite values.
Results may differ from a plain program's by a relative error of at most 0.015.
Values may be sent and summed in bfloat16 or wider, within the bound.
No kernel may reach another device: no remote copies, remote signals or barrier semaphores. Data moves between devices by JAX's collectives and lax.ppermute only.
A program may use at most 256 MiB of HBM per device.

v0:
```python
import jax
import jax.numpy as jnp
from jax import lax
from jax.sharding import PartitionSpec as P

HEADS = 10
HEAD_DIM = 64
FF = 2560
D = 640
FRAMES = 400
SPAN = 10
epsilon = 1e-05


def matmul(left, right):
    return jnp.dot(left, right, preferred_element_type=jnp.float32)


def matmul_nt(left, right):
    return lax.dot_general(
        left, right, (((1,), (1,)), ((), ())), preferred_element_type=jnp.float32
    )


def matmul_tn(left, right):
    return lax.dot_general(
        left, right, (((0,), (0,)), ((), ())), preferred_element_type=jnp.float32
    )


def layer_norm(value, gain, shift):
    center = value - jnp.mean(value, axis=-1, keepdims=True)
    spread = jnp.mean(center * center, axis=-1, keepdims=True)
    return center * lax.rsqrt(spread + epsilon) * gain + shift


def gelu_exact(value):
    return jax.nn.gelu(value, approximate=False)


def span_mask(starts):
    places = jnp.arange(FRAMES, dtype=jnp.int32)[None, :, None]
    inside = (places >= starts[:, None, :]) & (places < starts[:, None, :] + SPAN)
    return jnp.any(inside, axis=2)


def widen(grad, full_shape):
    return jnp.pad(grad, [(0, whole - part) for whole, part in zip(full_shape, grad.shape)])


def column_sum(value):
    return jnp.sum(value, axis=0, dtype=jnp.float32)


def cut_attn(gathered):
    query_w, key_w, value_w, out_w, query_b, value_b, out_b, gain_one, shift_one, mask_vec = (
        gathered
    )
    return (
        query_w[:D, :D],
        key_w[:D, :D],
        value_w[:D, :D],
        out_w[:D, :D],
        query_b[:D].astype(jnp.float32),
        value_b[:D].astype(jnp.float32),
        out_b[:D].astype(jnp.float32),
        gain_one[:D].astype(jnp.float32),
        shift_one[:D].astype(jnp.float32),
        mask_vec[:D].astype(jnp.float32),
    )


def cut_ffn(gathered):
    up_w, up_b, down_w, down_b, gain_two, shift_two = gathered
    return (
        up_w[:D, :FF],
        up_b[:FF].astype(jnp.float32),
        down_w[:FF, :D],
        down_b[:D].astype(jnp.float32),
        gain_two[:D].astype(jnp.float32),
        shift_two[:D].astype(jnp.float32),
    )


def on_device(
    frames,
    cotangent,
    span_starts,
    query_weight,
    key_weight,
    value_weight,
    out_weight,
    query_bias,
    value_bias,
    out_bias,
    first_gain,
    first_shift,
    up_weight,
    up_bias,
    down_weight,
    down_bias,
    second_gain,
    second_shift,
    mask_vector,
):
    attn_full = (
        lax.all_gather(query_weight, "fsdp", axis=0, tiled=True),
        lax.all_gather(key_weight, "fsdp", axis=0, tiled=True),
        lax.all_gather(value_weight, "fsdp", axis=0, tiled=True),
        lax.all_gather(out_weight, "fsdp", axis=0, tiled=True),
        lax.all_gather(query_bias, "fsdp", axis=0, tiled=True),
        lax.all_gather(value_bias, "fsdp", axis=0, tiled=True),
        lax.all_gather(out_bias, "fsdp", axis=0, tiled=True),
        lax.all_gather(first_gain, "fsdp", axis=0, tiled=True),
        lax.all_gather(first_shift, "fsdp", axis=0, tiled=True),
        lax.all_gather(mask_vector, "fsdp", axis=0, tiled=True),
    )
    attn_shapes = [piece.shape for piece in attn_full]
    query_w, key_w, value_w, out_w, query_b, value_b, out_b, gain_one, shift_one, mask_vec = (
        cut_attn(attn_full)
    )
    total_rows = frames.shape[0]
    utters = total_rows // FRAMES
    scale = HEAD_DIM ** (-0.5)
    masked = span_mask(span_starts).reshape(total_rows, 1)
    start_rows = jnp.where(masked, mask_vec[None, :], frames.astype(jnp.float32))
    start_low = start_rows.astype(jnp.bfloat16)
    query_rows = (matmul(start_low, query_w) + query_b).astype(jnp.bfloat16)
    key_rows = matmul(start_low, key_w).astype(jnp.bfloat16)
    value_rows = (matmul(start_low, value_w) + value_b).astype(jnp.bfloat16)
    query_heads = query_rows.reshape(utters, FRAMES, HEADS, HEAD_DIM)
    key_heads = key_rows.reshape(utters, FRAMES, HEADS, HEAD_DIM)
    value_heads = value_rows.reshape(utters, FRAMES, HEADS, HEAD_DIM)
    scores = (
        jnp.einsum("bqhd,bkhd->bhqk", query_heads, key_heads, preferred_element_type=jnp.float32)
        * scale
    )
    top = jnp.max(scores, axis=-1, keepdims=True)
    expo = jnp.exp(scores - top)
    total = jnp.sum(expo, axis=-1, keepdims=True)
    log_total = top + jnp.log(total)
    attn_prob = (expo / total).astype(jnp.bfloat16)
    mixed = jnp.einsum(
        "bhqk,bkhd->bqhd", attn_prob, value_heads, preferred_element_type=jnp.float32
    )
    mixed = mixed.reshape(total_rows, D).astype(jnp.bfloat16)
    branch_one = matmul(mixed, out_w) + out_b
    first_out, first_pull = jax.vjp(layer_norm, start_rows + branch_one, gain_one, shift_one)
    ffn_full = (
        lax.all_gather(up_weight, "fsdp", axis=0, tiled=True),
        lax.all_gather(up_bias, "fsdp", axis=0, tiled=True),
        lax.all_gather(down_weight, "fsdp", axis=0, tiled=True),
        lax.all_gather(down_bias, "fsdp", axis=0, tiled=True),
        lax.all_gather(second_gain, "fsdp", axis=0, tiled=True),
        lax.all_gather(second_shift, "fsdp", axis=0, tiled=True),
    )
    ffn_shapes = [piece.shape for piece in ffn_full]
    up_w, up_b, down_w, down_b, gain_two, shift_two = cut_ffn(ffn_full)
    first_low = first_out.astype(jnp.bfloat16)
    hidden_pre = matmul(first_low, up_w) + up_b
    hidden_act, gelu_pull = jax.vjp(gelu_exact, hidden_pre)
    hidden_low = hidden_act.astype(jnp.bfloat16)
    branch_two = matmul(hidden_low, down_w) + down_b
    result, second_pull = jax.vjp(layer_norm, first_out + branch_two, gain_two, shift_two)
    grad_two, grad_gain_two, grad_shift_two = second_pull(cotangent.astype(jnp.float32))
    grad_branch = grad_two.astype(jnp.bfloat16)
    ffn_back = cut_ffn(
        (
            lax.all_gather(up_weight, "fsdp", axis=0, tiled=True),
            lax.all_gather(up_bias, "fsdp", axis=0, tiled=True),
            lax.all_gather(down_weight, "fsdp", axis=0, tiled=True),
            lax.all_gather(down_bias, "fsdp", axis=0, tiled=True),
            lax.all_gather(second_gain, "fsdp", axis=0, tiled=True),
            lax.all_gather(second_shift, "fsdp", axis=0, tiled=True),
        )
    )
    up_w = ffn_back[0]
    down_w = ffn_back[2]
    grad_hidden = matmul_nt(grad_branch, down_w)
    (grad_pre,) = gelu_pull(grad_hidden)
    grad_pre_low = grad_pre.astype(jnp.bfloat16)
    grad_first = matmul_nt(grad_pre_low, up_w) + grad_two
    ffn_grads = (
        widen(matmul_tn(first_low, grad_pre_low), ffn_shapes[0]),
        widen(column_sum(grad_pre_low), ffn_shapes[1]),
        widen(matmul_tn(hidden_low, grad_branch), ffn_shapes[2]),
        widen(column_sum(grad_branch), ffn_shapes[3]),
        widen(grad_gain_two, ffn_shapes[4]),
        widen(grad_shift_two, ffn_shapes[5]),
    )
    grad_res, grad_gain_one, grad_shift_one = first_pull(grad_first)
    grad_attn_out = grad_res.astype(jnp.bfloat16)
    attn_back = cut_attn(
        (
            lax.all_gather(query_weight, "fsdp", axis=0, tiled=True),
            lax.all_gather(key_weight, "fsdp", axis=0, tiled=True),
            lax.all_gather(value_weight, "fsdp", axis=0, tiled=True),
            lax.all_gather(out_weight, "fsdp", axis=0, tiled=True),
            lax.all_gather(query_bias, "fsdp", axis=0, tiled=True),
            lax.all_gather(value_bias, "fsdp", axis=0, tiled=True),
            lax.all_gather(out_bias, "fsdp", axis=0, tiled=True),
            lax.all_gather(first_gain, "fsdp", axis=0, tiled=True),
            lax.all_gather(first_shift, "fsdp", axis=0, tiled=True),
            lax.all_gather(mask_vector, "fsdp", axis=0, tiled=True),
        )
    )
    query_w = attn_back[0]
    key_w = attn_back[1]
    value_w = attn_back[2]
    out_w = attn_back[3]
    grad_mixed = matmul_nt(grad_attn_out, out_w).astype(jnp.bfloat16)
    grad_mixed_heads = grad_mixed.reshape(utters, FRAMES, HEADS, HEAD_DIM)
    scores_again = (
        jnp.einsum("bqhd,bkhd->bhqk", query_heads, key_heads, preferred_element_type=jnp.float32)
        * scale
    )
    prob_again = jnp.exp(scores_again - log_total)
    grad_prob = jnp.einsum(
        "bqhd,bkhd->bhqk", grad_mixed_heads, value_heads, preferred_element_type=jnp.float32
    )
    grad_value = jnp.einsum(
        "bhqk,bqhd->bkhd",
        prob_again.astype(jnp.bfloat16),
        grad_mixed_heads,
        preferred_element_type=jnp.float32,
    )
    grad_value = grad_value.reshape(total_rows, D).astype(jnp.bfloat16)
    grad_scores = (
        prob_again * (grad_prob - jnp.sum(grad_prob * prob_again, axis=-1, keepdims=True))
    ).astype(jnp.bfloat16)
    grad_query = (
        jnp.einsum("bhqk,bkhd->bqhd", grad_scores, key_heads, preferred_element_type=jnp.float32)
        * scale
    )
    grad_query = grad_query.reshape(total_rows, D).astype(jnp.bfloat16)
    grad_key = (
        jnp.einsum("bhqk,bqhd->bkhd", grad_scores, query_heads, preferred_element_type=jnp.float32)
        * scale
    )
    grad_key = grad_key.reshape(total_rows, D).astype(jnp.bfloat16)
    grad_start = (
        matmul_nt(grad_query, query_w)
        + matmul_nt(grad_key, key_w)
        + matmul_nt(grad_value, value_w)
        + grad_res
    )
    frames_grad = jnp.where(masked, 0.0, grad_start).astype(jnp.bfloat16)
    grad_mask = jnp.sum(jnp.where(masked, grad_start, 0.0), axis=0)
    attn_grads = (
        widen(matmul_tn(start_low, grad_query), attn_shapes[0]),
        widen(matmul_tn(start_low, grad_key), attn_shapes[1]),
        widen(matmul_tn(start_low, grad_value), attn_shapes[2]),
        widen(matmul_tn(mixed, grad_attn_out), attn_shapes[3]),
        widen(column_sum(grad_query), attn_shapes[4]),
        widen(column_sum(grad_value), attn_shapes[5]),
        widen(column_sum(grad_attn_out), attn_shapes[6]),
        widen(grad_gain_one, attn_shapes[7]),
        widen(grad_shift_one, attn_shapes[8]),
        widen(grad_mask, attn_shapes[9]),
    )
    summed = lax.psum(
        (
            lax.psum_scatter(attn_grads[0], "fsdp", scatter_dimension=0, tiled=True),
            lax.psum_scatter(attn_grads[1], "fsdp", scatter_dimension=0, tiled=True),
            lax.psum_scatter(attn_grads[2], "fsdp", scatter_dimension=0, tiled=True),
            lax.psum_scatter(attn_grads[3], "fsdp", scatter_dimension=0, tiled=True),
            lax.psum_scatter(attn_grads[4], "fsdp", scatter_dimension=0, tiled=True),
            lax.psum_scatter(attn_grads[5], "fsdp", scatter_dimension=0, tiled=True),
            lax.psum_scatter(attn_grads[6], "fsdp", scatter_dimension=0, tiled=True),
            lax.psum_scatter(attn_grads[7], "fsdp", scatter_dimension=0, tiled=True),
            lax.psum_scatter(attn_grads[8], "fsdp", scatter_dimension=0, tiled=True),
            lax.psum_scatter(attn_grads[9], "fsdp", scatter_dimension=0, tiled=True),
            lax.psum_scatter(ffn_grads[0], "fsdp", scatter_dimension=0, tiled=True),
            lax.psum_scatter(ffn_grads[1], "fsdp", scatter_dimension=0, tiled=True),
            lax.psum_scatter(ffn_grads[2], "fsdp", scatter_dimension=0, tiled=True),
            lax.psum_scatter(ffn_grads[3], "fsdp", scatter_dimension=0, tiled=True),
            lax.psum_scatter(ffn_grads[4], "fsdp", scatter_dimension=0, tiled=True),
            lax.psum_scatter(ffn_grads[5], "fsdp", scatter_dimension=0, tiled=True),
        ),
        "dp",
    )
    attn_sums = summed[:10]
    ffn_sums = summed[10:]
    attn_sums = [piece for piece in attn_sums]
    ffn_sums = [piece for piece in ffn_sums]
    return (
        result.astype(jnp.bfloat16),
        frames_grad,
        attn_sums[0],
        attn_sums[1],
        attn_sums[2],
        attn_sums[3],
        attn_sums[4],
        attn_sums[5],
        attn_sums[6],
        attn_sums[7],
        attn_sums[8],
        ffn_sums[0],
        ffn_sums[1],
        ffn_sums[2],
        ffn_sums[3],
        ffn_sums[4],
        ffn_sums[5],
        attn_sums[9],
    )


def solution(mesh):
    return jax.shard_map(
        on_device,
        mesh=mesh,
        in_specs=(
            P(("dp", "fsdp"), None),
            P(("dp", "fsdp"), None),
            P(("dp", "fsdp"), None),
            P("fsdp", None),
            P("fsdp", None),
            P("fsdp", None),
            P("fsdp", None),
            P("fsdp"),
            P("fsdp"),
            P("fsdp"),
            P("fsdp"),
            P("fsdp"),
            P("fsdp", None),
            P("fsdp"),
            P("fsdp", None),
            P("fsdp"),
            P("fsdp"),
            P("fsdp"),
            P("fsdp"),
        ),
        out_specs=(
            P(("dp", "fsdp"), None),
            P(("dp", "fsdp"), None),
            P("fsdp", None),
            P("fsdp", None),
            P("fsdp", None),
            P("fsdp", None),
            P("fsdp"),
            P("fsdp"),
            P("fsdp"),
            P("fsdp"),
            P("fsdp"),
            P("fsdp", None),
            P("fsdp"),
            P("fsdp", None),
            P("fsdp"),
            P("fsdp"),
            P("fsdp"),
            P("fsdp"),
        ),
        check_vma=False,
    )
```

profile of v0, /device:TPU:0, one launch (start us, length us, event | category | flops | bytes accessed | tf_op | source)
XLA Modules:
  0.0 1117.5 jit_solution(11925511347061986627)
XLA Ops:
  23.0 39.2 %all-reduce.38 = (bf16[768]{0:T(1024)(128)(2,1)S(1)}, bf16[768]{0:T(1024)(128)(2,1)S(1)}, bf16[768]{0:T(1024)(128)(2,1)S(1)}, bf16[768]{0:T(1024)(128)(2,1)S(1)}...) all-reduce(bf16[768]{0:T(1024)(128)(2,1)S(1)} %dynamic-update-slice, ...), channel_id=1, replica_groups=mesh['dp'=4,'fsdp'=8] {'fsdp'}, use_global_device_ids=true, to_apply=%add.16 | all-reduce | flops 6912 | bytes 27648
  62.2 25.9 %all-gather = bf16[8,1,384]{2,1,0:T(2,128)(2,1)S(1)} all-gather(bf16[1,1,384]{2,1,0:T(2,128)(2,1)S(1)} %reshape.175), channel_id=1, replica_groups=mesh['dp'=4,'fsdp'=8] {'fsdp'}, dimensions={0}, use_global_device_ids=true | all-gather | bytes 6912 | tf_op jit(solution)/shard_map/all_gather | solution.py:151
  116.0 22.1 %all-gather.12.cloned.1.call-done = bf16[768,768]{1,0:T(8,128)(2,1)} async-done(((bf16[96,768]{1,0:T(8,128)(2,1)}), bf16[768,768]{1,0:T(8,128)(2,1)}) %all-gather.12.cloned.1.call-update) | async-done | bytes 1179664 | tf_op jit(solution)/shard_map/all_gather | solution.py:108
  152.4 15.5 %multiply_reduce_fusion.1 = (f32[4,10,400]{2,1,0:T(8,128)S(1)}, f32[4,10,400,400]{2,3,1,0:T(8,128)}) fusion(bf16[4,400,10,64]{1,0,3,2:T(4,128)(2,1)S(1)} %reshape.146, bf16[4,400,10,64]{1,0,3,2:T(4,128)(2,1)} %reshape.145), kind=kOutput, calls=%fused_computation.6 | convolution fusion | flops 831984000 | bytes 29760000 | tf_op jit(solution)/shard_map/bqhd,bkhd->bhqk/dot_general | solution.py:135
  167.9 14.0 %fusion = f32[4,10,400]{2,1,0:T(8,128)S(1)} fusion(f32[4,10,400,400]{2,3,1,0:T(8,128)} %get-tuple-element.73, f32[4,10,400]{2,1,0:T(8,128)S(1)} %get-tuple-element.72), kind=kLoop, calls=%fused_computation.5 | loop fusion | flops 19184000 | bytes 25728000 | tf_op jit(solution)/shard_map/reduce_sum | solution.py:140
  182.0 16.0 %convert_bitcast_fusion = bf16[4,400,10,64]{1,3,2,0:T(8,128)(2,1)} fusion(f32[4,10,400,400]{2,3,1,0:T(8,128)} %get-tuple-element.73, f32[4,10,400]{2,1,0:T(8,128)S(1)} %fusion, f32[4,10,400]{2,1,0:T(8,128)S(1)} %get-tuple-element.72, bf16[4,400,10,64]{1,0,3,2:T(4,128)(2,1)S(1)} %copy-done.8), kind=kOutput, calls=%fused_computation.72 | convolution fusion | flops 845824000 | bytes 29824000 | tf_op jit(solution)/shard_map/bhqk,bkhd->bqhd/dot_general | solution.py:143
  213.5 47.2 %all-gather.16.cloned.1.call-done = bf16[768,3072]{1,0:T(8,128)(2,1)} async-done(((bf16[96,3072]{1,0:T(8,128)(2,1)}), bf16[768,3072]{1,0:T(8,128)(2,1)}) %all-gather.16.cloned.1.call-update) | async-done | bytes 4718608 | tf_op jit(solution)/shard_map/all_gather | solution.py:150
  260.8 46.6 %multiply_convert_fusion.1 = (bf16[1600,2560]{1,0:T(8,128)(2,1)}, f32[1600,2560]{1,0:T(8,128)}, f32[1600,2560]{1,0:T(8,128)}) fusion(f32[2560]{0:T(1024)S(1)} %slice_convert_fusion, bf16[768,3072]{1,0:T(8,128)(2,1)} %all-gather.16.cloned.1.call-done, f32[1600,640]{1,0:T(8,128)} %copy-done.5, f32[640]{0:T(1024)S(1)} %get-tuple-element.93, ...), kind=kOutput, calls=%fused_computation.14 | convolution fusion | flops 5518336000 | bytes 48360960 | tf_op jit(solution)/shard_map/dot_general | solution.py:16
  307.4 33.5 %all-gather.18.cloned.1.call-done = bf16[3072,768]{1,0:T(8,128)(2,1)} async-done(((bf16[384,768]{1,0:T(8,128)(2,1)}), bf16[3072,768]{1,0:T(8,128)(2,1)}) %all-gather.18.cloned.1.call-update) | async-done | bytes 4718608 | tf_op jit(solution)/shard_map/all_gather | solution.py:152
  340.9 12.8 %fusion.81 = (f32[1600]{0:T(1024)S(1)}, f32[1600,640]{1,0:T(8,128)S(1)}) fusion(f32[640]{0:T(1024)S(1)} %copy-done.34, bf16[1600,2560]{1,0:T(8,128)(2,1)} %get-tuple-element.67, bf16[3072,768]{1,0:T(8,128)(2,1)} %all-gather.18.cloned.1.call-done, f32[640]{0:T(1024)S(1)} %get-tuple-element.93, f32[640]{0:T(1024)S(1)} %slice_convert_fusion.5, ...), kind=kOutput, calls=%fused_computation.132 | convolution fusion | flops 5250046464 | bytes 19687680 | tf_op jit(solution)/shard_map/dot_general | solution.py:16
  363.5 21.7 %convert_reduce_fusion = (f32[2560]{0:T(1024)}, bf16[1600,2560]{1,0:T(8,128)(2,1)}) fusion(f32[1600,2560]{1,0:T(8,128)} %get-tuple-element.68, bf16[1600,640]{1,0:T(8,128)(2,1)S(1)} %get-tuple-element.60, bf16[3072,768]{1,0:T(8,128)(2,1)} %all-gather.18.cloned.1.call-done, f32[1600,2560]{1,0:T(8,128)} %get-tuple-element.76, f32[2560]{0:T(1024)S(1)} %slice_convert_fusion), kind=kOutput, calls=%fused_computation.11 | convolution fusion | flops 5312509440 | bytes 46305280 | tf_op jit(solution)/shard_map/dot_general | solution.py:20
  385.2 14.5 %multiply_reduce_fusion.2 = (f32[640]{0:T(1024)S(1)}, f32[1600]{0:T(1024)S(1)}, f32[640]{0:T(1024)S(1)}, f32[1600,640]{1,0:T(8,128)S(1)}) fusion(f32[1600,640]{1,0:T(8,128)} %copy-done.5, f32[1600]{0:T(1024)S(1)} %fusion.60, f32[1600]{0:T(1024)S(1)} %broadcast_multiply_fusion.1, f32[640]{0:T(1024)S(1)} %slice_convert_fusion.5, f32[1600,640]{1,0:T(8,128)} %copy-done.7, ...), kind=kOutput, calls=%fused_computation.45 | convolution fusion | flops 5253117440 | bytes 23790080 | tf_op jit(solution)/shard_map/dot_general | solution.py:20
  422.8 15.7 %convert_reduce_fusion.2 = (f32[10,64]{1,0:T(8,128)S(1)}, bf16[4,10,64,400]{3,2,1,0:T(8,128)(2,1)}) fusion(f32[4,10,400,400]{2,3,1,0:T(8,128)} %get-tuple-element.73, f32[4,10,400]{2,1,0:T(8,128)S(1)} %log_add_fusion, bf16[4,400,10,64]{1,0,3,2:T(4,128)(2,1)S(1)} %reshape.147), kind=kOutput, calls=%fused_computation.35 | convolution fusion | flops 841471360 | bytes 29762560 | tf_op jit(solution)/shard_map/bhqk,bqhd->bkhd/dot_general | solution.py:221
  456.0 25.6 %multiply_reduce_fusion = (f32[4,10,400]{2,1,0:T(8,128)S(1)}, f32[4,10,400,400]{2,3,1,0:T(8,128)}) fusion(f32[4,10,400,400]{2,3,1,0:T(8,128)} %get-tuple-element.73, f32[4,10,400]{2,1,0:T(8,128)S(1)} %log_add_fusion, bf16[4,400,10,64]{1,0,3,2:T(4,128)(2,1)} %reshape.144, bf16[4,400,10,64]{1,0,3,2:T(4,128)(2,1)S(1)} %reshape.147), kind=kOutput, calls=%fused_computation.1 | convolution fusion | flops 844784000 | bytes 55424000 | tf_op jit(solution)/shard_map/bqhd,bkhd->bhqk/dot_general | solution.py:218
  481.6 28.0 %multiply_convert_fusion = bf16[4,10,400,400]{2,3,1,0:T(8,128)(2,1)} fusion(f32[4,10,400,400]{2,3,1,0:T(8,128)} %get-tuple-element.81, f32[4,10,400,400]{2,3,1,0:T(8,128)} %get-tuple-element.73, f32[4,10,400]{2,1,0:T(8,128)S(1)} %get-tuple-element.80, f32[4,10,400]{2,1,0:T(8,128)S(1)} %log_add_fusion), kind=kLoop, calls=%fused_computation | loop fusion | flops 32000000 | bytes 64128000 | tf_op jit(solution)/shard_map/convert_element_type | solution.py:230
  531.1 9.0 convert_reduce_fusion.3
  551.9 10.6 fusion.64
  568.9 9.9 fusion.83
  584.6 34.2 %reduce-scatter.9.cloned.1.call-done = f32[96,768]{1,0:T(8,128)} async-done(((f32[768,768]{1,0:T(8,128)}), f32[96,768]{1,0:T(8,128)}) %reduce-scatter.9.cloned.1.call-update) | async-done | bytes 294928 | tf_op jit(solution)/shard_map/reduce_scatter | solution.py:264
  618.9 71.5 %reduce-scatter.7.cloned.1.call-done = f32[96,768]{1,0:T(8,128)} async-done(((f32[768,768]{1,0:T(8,128)}), f32[96,768]{1,0:T(8,128)}) %reduce-scatter.7.cloned.1.call-update) | async-done | bytes 294928 | tf_op jit(solution)/shard_map/reduce_scatter | solution.py:263
  690.3 166.1 %reduce-scatter.15.cloned.1.call-done = f32[96,3072]{1,0:T(8,128)} async-done(((f32[768,3072]{1,0:T(8,128)}), f32[96,3072]{1,0:T(8,128)}) %reduce-scatter.15.cloned.1.call-update) | async-done | bytes 1179664 | tf_op jit(solution)/shard_map/reduce_scatter | solution.py:273
  856.4 166.1 %reduce-scatter.17.cloned.1.call-done = f32[384,768]{1,0:T(8,128)} async-done(((f32[3072,768]{1,0:T(8,128)}), f32[384,768]{1,0:T(8,128)}) %reduce-scatter.17.cloned.1.call-update) | async-done | bytes 1179664 | tf_op jit(solution)/shard_map/reduce_scatter | solution.py:275
  1039.9 35.3 %all-reduce.35 = (f32[768]{0:T(1024)S(1)}, f32[768]{0:T(1024)S(1)}, f32[768]{0:T(1024)S(1)}, f32[768]{0:T(1024)S(1)}, f32[768]{0:T(1024)S(1)}, /*index=5*/f32[30...) all-reduce(f32[768]{0:T(1024)S(1)} %pad.57, ...), channel_id=6, replica_groups=mesh['dp'=4,'fsdp'=8] {'fsdp'}, use_global_device_ids=true, to_apply=%region_21.22.clone | all-reduce | flops 9984 | bytes 79872
  1082.9 17.5 %all-reduce.41.cloned.1.call-done = (f32[96,768]{1,0:T(8,128)}, f32[96,768]{1,0:T(8,128)}, f32[96,768]{1,0:T(8,128)}, f32[96,768]{1,0:T(8,128)}, f32[96,3072]{1,0:T(8,128)}, /*index=5*/f32[384,768]{1,0:T(8,128)}) async-done(((f32[96,768]{1,0:T(8,128)}, f32[96,768]{1,0:T(8,128)}, f32[96,768]{1,0:T(8,128)}, f32[96,768]{1,0:T(8,128)}, f32[96,3072]{1,0:T(8,128)}, /*index=5*/f32[384,768]{1,0:T(8,128)}), ...) | async-done | bytes 3538960 | tf_op jit(solution)/shard_map/psum | solution.py:261
  (219 shorter events, 202.1 us)
Async XLA Ops:
  7.2 82.3 %all-gather.8.cloned.1.call-start = ((), (), s32[]{:S(2)}) async-start(), calls=%async_computation.6 | async-start | bytes 1327104 | tf_op jit(solution)/shard_map/all_gather | solution.py:109
  7.9 95.0 %all-gather.10.cloned.1.call-start = ((), (), s32[]{:S(2)}) async-start(), calls=%async_computation.7 | async-start | bytes 1327104 | tf_op jit(solution)/shard_map/all_gather | solution.py:107
  8.7 129.4 %all-gather.12.cloned.1.call-start = ((), (), s32[]{:S(2)}) async-start(), calls=%async_computation.8 | async-start | bytes 1327104 | tf_op jit(solution)/shard_map/all_gather | solution.py:108
  9.4 195.8 %all-gather.14.cloned.1.call-start = ((), (), s32[]{:S(2)}) async-start(), calls=%async_computation.9 | async-start | bytes 1327104 | tf_op jit(solution)/shard_map/all_gather | solution.py:110
  10.0 250.8 %all-gather.16.cloned.1.call-start = ((), (), s32[]{:S(2)}) async-start(), calls=%async_computation.10 | async-start | bytes 5308416 | tf_op jit(solution)/shard_map/all_gather | solution.py:150
  10.6 330.3 %all-gather.18.cloned.1.call-start = ((), (), s32[]{:S(2)}) async-start(), calls=%async_computation.11 | async-start | bytes 5308416 | tf_op jit(solution)/shard_map/all_gather | solution.py:152
  11.1 573.4 %reduce-scatter.13.cloned.1.call-start = ((), (), s32[]{:S(2)}) async-start(), calls=%async_computation.15 | async-start | bytes 2654208 | tf_op jit(solution)/shard_map/reduce_scatter | solution.py:266
  13.5 191.7 %copy-start.25 = (pred[1600]{0:T(1024)(128)(4,1)}, pred[1600]{0:T(1024)(128)(4,1)S(1)}, u32[]{:S(2)}) copy-start(pred[1600]{0:T(1024)(128)(4,1)S(1)} %broadcast_in_dim.36) | copy-start | bytes 4804
  62.2 143.0 %copy-start.35 = (f32[640]{0:T(1024)}, f32[640]{0:T(1024)S(1)}, u32[]{:S(2)}) copy-start(f32[640]{0:T(1024)S(1)} %slice_convert_fusion.9) | copy-start | bytes 7684
  88.9 252.0 %copy-start.32 = (f32[640]{0:T(1024)}, f32[640]{0:T(1024)S(1)}, u32[]{:S(2)}) copy-start(f32[640]{0:T(1024)S(1)} %get-tuple-element.93) | copy-start | bytes 7684
  152.4 15.5 %copy-start.2 = (bf16[4,400,10,64]{1,0,3,2:T(4,128)(2,1)}, bf16[4,400,10,64]{1,0,3,2:T(4,128)(2,1)S(1)}, u32[]{:S(2)}) copy-start(bf16[4,400,10,64]{1,0,3,2:T(4,128)(2,1)S(1)} %reshape.146) | copy-start | bytes 6144004
  167.9 14.1 %copy-start.8 = (bf16[4,400,10,64]{1,0,3,2:T(4,128)(2,1)S(1)}, bf16[4,400,10,64]{1,0,3,2:T(4,128)(2,1)}, u32[]{:S(2)}) copy-start(bf16[4,400,10,64]{1,0,3,2:T(4,128)(2,1)} %reshape.144) | copy-start | bytes 6144004
  181.9 16.0 %copy-start.20 = (f32[4,10,400]{2,1,0:T(8,128)}, f32[4,10,400]{2,1,0:T(8,128)S(1)}, u32[]{:S(2)}) copy-start(f32[4,10,400]{2,1,0:T(8,128)S(1)} %fusion) | copy-start | bytes 192004
  260.8 80.1 %copy-start.34 = (f32[640]{0:T(1024)S(1)}, f32[640]{0:T(1024)}, u32[]{:S(2)}) copy-start(f32[640]{0:T(1024)} %get-tuple-element.92) | copy-start | bytes 7684
  363.5 21.7 %copy-start.13 = (bf16[1600,640]{1,0:T(8,128)(2,1)}, bf16[1600,640]{1,0:T(8,128)(2,1)S(1)}, u32[]{:S(2)}) copy-start(bf16[1600,640]{1,0:T(8,128)(2,1)S(1)} %get-tuple-element.60) | copy-start | bytes 6144004
  385.2 14.5 %copy-start.23 = (f32[1600]{0:T(1024)S(1)}, f32[1600]{0:T(1024)}, u32[]{:S(2)}) copy-start(f32[1600]{0:T(1024)} %copy-done.22) | copy-start | bytes 19204
  385.2 14.6 %copy-start.6 = (f32[1600,640]{1,0:T(8,128)S(1)}, f32[1600,640]{1,0:T(8,128)}, u32[]{:S(2)}) copy-start(f32[1600,640]{1,0:T(8,128)} %copy-done.5) | copy-start | bytes 12288004
  408.2 176.4 %reduce-scatter.11.cloned.1.call-start = ((), (), s32[]{:S(2)}) async-start(), calls=%async_computation.14 | async-start | bytes 2654208 | tf_op jit(solution)/shard_map/reduce_scatter | solution.py:265
  456.0 162.9 %reduce-scatter.9.cloned.1.call-start = ((), (), s32[]{:S(2)}) async-start(), calls=%async_computation.13 | async-start | bytes 2654208 | tf_op jit(solution)/shard_map/reduce_scatter | solution.py:264
  481.6 28.0 %copy-start.4 = (bf16[4,400,10,64]{1,0,3,2:T(4,128)(2,1)S(1)}, bf16[4,400,10,64]{1,0,3,2:T(4,128)(2,1)}, u32[]{:S(2)}) copy-start(bf16[4,400,10,64]{1,0,3,2:T(4,128)(2,1)} %reshape.145) | copy-start | bytes 6144004
  530.2 160.2 %reduce-scatter.7.cloned.1.call-start = ((), (), s32[]{:S(2)}) async-start(), calls=%async_computation.12 | async-start | bytes 2654208 | tf_op jit(solution)/shard_map/reduce_scatter | solution.py:263
  551.9 304.5 %reduce-scatter.15.cloned.1.call-start = ((), (), s32[]{:S(2)}) async-start(), calls=%async_computation.16 | async-start | bytes 10616832 | tf_op jit(solution)/shard_map/reduce_scatter | solution.py:273
  567.4 455.1 %reduce-scatter.17.cloned.1.call-start = ((), (), s32[]{:S(2)}) async-start(), calls=%async_computation.17 | async-start | bytes 10616832 | tf_op jit(solution)/shard_map/reduce_scatter | solution.py:275
  583.2 517.3 %all-reduce.41.cloned.1.call-start = ((), (), s32[]{:S(2)}) async-start(), calls=%async_computation.18 | async-start | bytes 7077888 | tf_op jit(solution)/shard_map/psum | solution.py:261
  (26 other events, 120.0 us)
Sparse Core Ops, SparseCore 0:
  10.2 43.8 all-gather.7
  56.3 39.6 all-gather.9
  98.2 39.8 all-gather.11
  140.1 39.8 all-gather.13
  182.0 78.6 all-gather.15
  262.8 78.0 all-gather.17
  408.3 67.1 reduce-scatter.12
  479.0 68.0 reduce-scatter.10
  550.6 68.2 reduce-scatter.8
  622.2 68.0 reduce-scatter.6
  693.9 162.4 reduce-scatter.14
  859.9 162.5 reduce-scatter.16
  1025.3 75.1 all-reduce.40
where the time goes:
time: 1120 us
  waiting for transfers between devices  562 us (50%)
  matrix products  261 us (23%)
  local copies, waits for them, and re-layouts  114 us (10%)
  blocking collectives  107 us (10%)
  other arithmetic  55 us (5%)
  between operations  16.8 us (2%)
    reduce_scatter x1, waiting for transfers between devices, on_device(): lax.psum_scatter(ffn_grads[0], 'fsdp', scatter_dimension=0, tiled=True)  166 us
    reduce_scatter x1, waiting for transfers between devices, on_device(): lax.psum_scatter(ffn_grads[2], 'fsdp', scatter_dimension=0, tiled=True)  166 us
    dot_general x6, matrix products, matmul(): return jnp.dot(left, right, preferred_element_type=jnp.float32)  78.6 us
    unnamed x2, blocking collectives  74.5 us
    reduce_scatter x1, waiting for transfers between devices, on_device(): lax.psum_scatter(attn_grads[0], 'fsdp', scatter_dimension=0, tiled=True)  71.5 us
    dot_general x6, matrix products, matmul_nt(): lax.dot_general(left, right, (((1,), (1,)), ((), ())), preferred_element_...  56.2 us
    all_gather x1, waiting for transfers between devices, on_device(): lax.all_gather(up_weight, 'fsdp', axis=0, tiled=True)  47.2 us
    dot_general x6, matrix products, matmul_tn(): lax.dot_general(left, right, (((0,), (0,)), ((), ())), preferred_element_...  36.2 us
  transfers between devices with their start and end apart: 13, of which 8 were waited for; matrix products, arithmetic and copies ran while one was open for 31% of the time, Pallas kernels for 0%

commit v1 on v0

--- a/solution.py
+++ b/solution.py
@@ -1,7 +1,9 @@
+import functools
 import jax
 import jax.numpy as jnp
 from jax import lax
 from jax.sharding import PartitionSpec as P
+from jax.lax import axis_index, ppermute, psum
 
 HEADS = 10
 HEAD_DIM = 64
@@ -10,6 +12,28 @@
 FRAMES = 400
 SPAN = 10
 epsilon = 1e-05
+
+
+def attach_chunk(frame_in, lane_axis, d0):
+    ready, local_out, newest = (psum(1, lane_axis), axis_index(lane_axis), frame_in.shape[d0])
+    block_out, block_last = (frame_in, 1)
+    while block_last < ready:
+        block_out = jnp.concatenate(
+            [
+                block_out,
+                ppermute(
+                    block_out,
+                    lane_axis,
+                    tuple(((src_i, (src_i - block_last) % ready) for src_i in range(ready))),
+                ),
+            ],
+            axis=d0,
+        )
+        block_last = 2 * block_last
+    return jnp.roll(block_out, local_out * newest, d0)
+
+
+_order_ways = functools.partial(attach_chunk, lane_axis="fsdp", d0=0)
 
 
 def matmul(left, right):
@@ -148,7 +172,7 @@
     first_out, first_pull = jax.vjp(layer_norm, start_rows + branch_one, gain_one, shift_one)
     ffn_full = (
         lax.all_gather(up_weight, "fsdp", axis=0, tiled=True),
-        lax.all_gather(up_bias, "fsdp", axis=0, tiled=True),
+        _order_ways(up_bias),
         lax.all_gather(down_weight, "fsdp", axis=0, tiled=True),
         lax.all_gather(down_bias, "fsdp", axis=0, tiled=True),
         lax.all_gather(second_gain, "fsdp", axis=0, tiled=True),

time: 1120 us -> 1120 us (level)
  blocking collectives: 107 us -> 75.8 us
  waiting for transfers between devices: 562 us -> 584 us
    all_gather x1 -> x0, blocking collectives: 25.9 us -> none  [on_device(): lax.all_gather(up_bias, 'fsdp', axis=0, tiled=True)]
    unnamed x111 -> x116, local copies, waits for them, and re-layouts: 31.1 us -> 33 us
  transfers between devices with their start and end apart: 13 -> 16, of which waited for: 8 -> 11; matrix products, arithmetic and copies ran while one was open for 31% -> 31% of each run, Pallas kernels for 0% -> 0%
where the time goes in v1:
time: 1120 us
  waiting for transfers between devices  584 us (52%)
  matrix products  261 us (23%)
  local copies, waits for them, and re-layouts  116 us (10%)
  blocking collectives  75.8 us (7%)
  other arithmetic  56.3 us (5%)
  between operations  16.8 us (2%)
    reduce_scatter x1, waiting for transfers between devices, on_device(): lax.psum_scatter(ffn_grads[0], 'fsdp', scatter_dimension=0, tiled=True)  166 us
    reduce_scatter x1, waiting for transfers between devices, on_device(): lax.psum_scatter(ffn_grads[2], 'fsdp', scatter_dimension=0, tiled=True)  166 us
    dot_general x6, matrix products, matmul(): return jnp.dot(left, right, preferred_element_type=jnp.float32)  78.1 us
    reduce_scatter x1, waiting for transfers between devices, on_device(): lax.psum_scatter(attn_grads[0], 'fsdp', scatter_dimension=0, tiled=True)  71.4 us
    unnamed x2, blocking collectives  68.8 us
    dot_general x6, matrix products, matmul_nt(): lax.dot_general(left, right, (((1,), (1,)), ((), ())), preferred_element_...  56.3 us
    all_gather x1, waiting for transfers between devices, on_device(): lax.all_gather(up_weight, 'fsdp', axis=0, tiled=True)  46.6 us
    dot_general x6, matrix products, matmul_tn(): lax.dot_general(left, right, (((0,), (0,)), ((), ())), preferred_element_...  36.2 us
  transfers between devices with their start and end apart: 16, of which 11 were waited for; matrix products, arithmetic and copies ran while one was open for 31% of the time, Pallas kernels for 0%

profile of v1, /device:TPU:0, one launch (start us, length us, event | category | flops | bytes accessed | tf_op | source)
XLA Modules:
  0.0 1117.4 jit_solution(13873584803537019782)
XLA Ops:
  26.3 33.5 %all-reduce.38 = (bf16[768]{0:T(1024)(128)(2,1)S(1)}, bf16[768]{0:T(1024)(128)(2,1)S(1)}, bf16[768]{0:T(1024)(128)(2,1)S(1)}, bf16[768]{0:T(1024)(128)(2,1)S(1)}...) all-reduce(bf16[768]{0:T(1024)(128)(2,1)S(1)} %dynamic-update-slice, ...), channel_id=1, replica_groups=mesh['dp'=4,'fsdp'=8] {'fsdp'}, use_global_device_ids=true, to_apply=%add.16 | all-reduce | flops 6912 | bytes 27648
  85.5 10.8 all-gather.9.cloned.1.call-done
  109.4 29.0 %all-gather.11.cloned.1.call-done = bf16[768,768]{1,0:T(8,128)(2,1)} async-done(((bf16[96,768]{1,0:T(8,128)(2,1)}), bf16[768,768]{1,0:T(8,128)(2,1)}) %all-gather.11.cloned.1.call-update) | async-done | bytes 1179664 | tf_op jit(solution)/shard_map/all_gather | solution.py:132
  152.9 15.4 %multiply_reduce_fusion.1 = (f32[4,10,400]{2,1,0:T(8,128)S(1)}, f32[4,10,400,400]{2,3,1,0:T(8,128)}) fusion(bf16[4,400,10,64]{1,0,3,2:T(4,128)(2,1)S(1)} %reshape.146, bf16[4,400,10,64]{1,0,3,2:T(4,128)(2,1)} %reshape.145), kind=kOutput, calls=%fused_computation.6 | convolution fusion | flops 831984000 | bytes 29760000 | tf_op jit(solution)/shard_map/bqhd,bkhd->bhqk/dot_general | solution.py:159
  168.3 14.0 %fusion = f32[4,10,400]{2,1,0:T(8,128)S(1)} fusion(f32[4,10,400,400]{2,3,1,0:T(8,128)} %get-tuple-element.73, f32[4,10,400]{2,1,0:T(8,128)S(1)} %get-tuple-element.72), kind=kLoop, calls=%fused_computation.5 | loop fusion | flops 19184000 | bytes 25728000 | tf_op jit(solution)/shard_map/reduce_sum | solution.py:164
  182.3 16.0 %convert_bitcast_fusion = bf16[4,400,10,64]{1,3,2,0:T(8,128)(2,1)} fusion(f32[4,10,400,400]{2,3,1,0:T(8,128)} %get-tuple-element.73, f32[4,10,400]{2,1,0:T(8,128)S(1)} %fusion, f32[4,10,400]{2,1,0:T(8,128)S(1)} %get-tuple-element.72, bf16[4,400,10,64]{1,0,3,2:T(4,128)(2,1)S(1)} %copy-done.8), kind=kOutput, calls=%fused_computation.72 | convolution fusion | flops 845824000 | bytes 29824000 | tf_op jit(solution)/shard_map/bhqk,bkhd->bqhd/dot_general | solution.py:167
  214.4 46.6 %all-gather.15.cloned.1.call-done = bf16[768,3072]{1,0:T(8,128)(2,1)} async-done(((bf16[96,3072]{1,0:T(8,128)(2,1)}), bf16[768,3072]{1,0:T(8,128)(2,1)}) %all-gather.15.cloned.1.call-update) | async-done | bytes 4718608 | tf_op jit(solution)/shard_map/all_gather | solution.py:174
  261.0 46.2 %multiply_convert_fusion.1 = (bf16[1600,2560]{1,0:T(8,128)(2,1)}, f32[1600,2560]{1,0:T(8,128)}, f32[1600,2560]{1,0:T(8,128)}) fusion(f32[2560]{0:T(1024)S(1)} %dynamic-slice_convert_fusion, bf16[768,3072]{1,0:T(8,128)(2,1)} %all-gather.15.cloned.1.call-done, f32[1600,640]{1,0:T(8,128)} %copy-done.5, f32[640]{0:T(1024)S(1)} %get-tuple-element.92, ...), kind=kOutput, calls=%fused_computation.14 | convolution fusion | flops 5518336000 | bytes 48360960 | tf_op jit(solution)/shard_map/dot_general | solution.py:40
  307.2 33.9 %all-gather.17.cloned.1.call-done = bf16[3072,768]{1,0:T(8,128)(2,1)} async-done(((bf16[384,768]{1,0:T(8,128)(2,1)}), bf16[3072,768]{1,0:T(8,128)(2,1)}) %all-gather.17.cloned.1.call-update) | async-done | bytes 4718608 | tf_op jit(solution)/shard_map/all_gather | solution.py:176
  341.1 12.8 %fusion.81 = (f32[1600]{0:T(1024)S(1)}, f32[1600,640]{1,0:T(8,128)S(1)}) fusion(f32[640]{0:T(1024)S(1)} %copy-done.36, bf16[1600,2560]{1,0:T(8,128)(2,1)} %get-tuple-element.67, bf16[3072,768]{1,0:T(8,128)(2,1)} %all-gather.17.cloned.1.call-done, f32[640]{0:T(1024)S(1)} %get-tuple-element.92, f32[640]{0:T(1024)S(1)} %get-tuple-element.93, ...), kind=kOutput, calls=%fused_computation.134 | convolution fusion | flops 5250046464 | bytes 19687680 | tf_op jit(solution)/shard_map/dot_general | solution.py:40
  363.8 21.9 %convert_reduce_fusion = (f32[2560]{0:T(1024)}, bf16[1600,2560]{1,0:T(8,128)(2,1)}) fusion(f32[1600,2560]{1,0:T(8,128)} %get-tuple-element.68, bf16[1600,640]{1,0:T(8,128)(2,1)S(1)} %get-tuple-element.60, bf16[3072,768]{1,0:T(8,128)(2,1)} %all-gather.17.cloned.1.call-done, f32[1600,2560]{1,0:T(8,128)} %get-tuple-element.76, ...), kind=kOutput, calls=%fused_computation.11 | convolution fusion | flops 5312509440 | bytes 46305280 | tf_op jit(solution)/shard_map/dot_general | solution.py:44
  385.7 14.5 %multiply_reduce_fusion.2 = (f32[640]{0:T(1024)S(1)}, f32[1600]{0:T(1024)S(1)}, f32[640]{0:T(1024)S(1)}, f32[1600,640]{1,0:T(8,128)S(1)}) fusion(f32[1600,640]{1,0:T(8,128)} %copy-done.5, f32[1600]{0:T(1024)S(1)} %fusion.60, f32[1600]{0:T(1024)S(1)} %broadcast_multiply_fusion.1, f32[640]{0:T(1024)S(1)} %get-tuple-element.93, f32[1600,640]{1,0:T(8,128)} %copy-done.7, ...), kind=kOutput, calls=%fused_computation.45 | convolution fusion | flops 5253117440 | bytes 23790080 | tf_op jit(solution)/shard_map/dot_general | solution.py:44
  423.2 15.7 %convert_reduce_fusion.2 = (f32[10,64]{1,0:T(8,128)S(1)}, bf16[4,10,64,400]{3,2,1,0:T(8,128)(2,1)}) fusion(f32[4,10,400,400]{2,3,1,0:T(8,128)} %get-tuple-element.73, f32[4,10,400]{2,1,0:T(8,128)S(1)} %log_add_fusion, bf16[4,400,10,64]{1,0,3,2:T(4,128)(2,1)S(1)} %reshape.147), kind=kOutput, calls=%fused_computation.35 | convolution fusion | flops 841471360 | bytes 29762560 | tf_op jit(solution)/shard_map/bhqk,bqhd->bkhd/dot_general | solution.py:245
  456.5 25.4 %multiply_reduce_fusion = (f32[4,10,400]{2,1,0:T(8,128)S(1)}, f32[4,10,400,400]{2,3,1,0:T(8,128)}) fusion(f32[4,10,400,400]{2,3,1,0:T(8,128)} %get-tuple-element.73, f32[4,10,400]{2,1,0:T(8,128)S(1)} %log_add_fusion, bf16[4,400,10,64]{1,0,3,2:T(4,128)(2,1)} %reshape.144, bf16[4,400,10,64]{1,0,3,2:T(4,128)(2,1)S(1)} %reshape.147), kind=kOutput, calls=%fused_computation.1 | convolution fusion | flops 844784000 | bytes 55424000 | tf_op jit(solution)/shard_map/bqhd,bkhd->bhqk/dot_general | solution.py:242
  481.9 28.0 %multiply_convert_fusion = bf16[4,10,400,400]{2,3,1,0:T(8,128)(2,1)} fusion(f32[4,10,400,400]{2,3,1,0:T(8,128)} %get-tuple-element.81, f32[4,10,400,400]{2,3,1,0:T(8,128)} %get-tuple-element.73, f32[4,10,400]{2,1,0:T(8,128)S(1)} %get-tuple-element.80, f32[4,10,400]{2,1,0:T(8,128)S(1)} %log_add_fusion), kind=kLoop, calls=%fused_computation | loop fusion | flops 32000000 | bytes 64128000 | tf_op jit(solution)/shard_map/convert_element_type | solution.py:254
  531.4 9.0 convert_reduce_fusion.3
  552.2 10.6 fusion.64
  569.3 9.9 fusion.83
  584.9 34.1 %reduce-scatter.9.cloned.1.call-done = f32[96,768]{1,0:T(8,128)} async-done(((f32[768,768]{1,0:T(8,128)}), f32[96,768]{1,0:T(8,128)}) %reduce-scatter.9.cloned.1.call-update) | async-done | bytes 294928 | tf_op jit(solution)/shard_map/reduce_scatter | solution.py:288
  619.1 71.4 %reduce-scatter.7.cloned.1.call-done = f32[96,768]{1,0:T(8,128)} async-done(((f32[768,768]{1,0:T(8,128)}), f32[96,768]{1,0:T(8,128)}) %reduce-scatter.7.cloned.1.call-update) | async-done | bytes 294928 | tf_op jit(solution)/shard_map/reduce_scatter | solution.py:287
  690.4 166.1 %reduce-scatter.15.cloned.1.call-done = f32[96,3072]{1,0:T(8,128)} async-done(((f32[768,3072]{1,0:T(8,128)}), f32[96,3072]{1,0:T(8,128)}) %reduce-scatter.15.cloned.1.call-update) | async-done | bytes 1179664 | tf_op jit(solution)/shard_map/reduce_scatter | solution.py:297
  856.5 165.9 %reduce-scatter.17.cloned.1.call-done = f32[384,768]{1,0:T(8,128)} async-done(((f32[3072,768]{1,0:T(8,128)}), f32[384,768]{1,0:T(8,128)}) %reduce-scatter.17.cloned.1.call-update) | async-done | bytes 1179664 | tf_op jit(solution)/shard_map/reduce_scatter | solution.py:299
  1039.8 35.3 %all-reduce.35 = (f32[768]{0:T(1024)S(1)}, f32[768]{0:T(1024)S(1)}, f32[768]{0:T(1024)S(1)}, f32[768]{0:T(1024)S(1)}, f32[768]{0:T(1024)S(1)}, /*index=5*/f32[30...) all-reduce(f32[768]{0:T(1024)S(1)} %pad.57, ...), channel_id=6, replica_groups=mesh['dp'=4,'fsdp'=8] {'fsdp'}, use_global_device_ids=true, to_apply=%region_21.22.clone | all-reduce | flops 9984 | bytes 79872
  1082.8 17.6 %all-reduce.41.cloned.1.call-done = (f32[96,768]{1,0:T(8,128)}, f32[96,768]{1,0:T(8,128)}, f32[96,768]{1,0:T(8,128)}, f32[96,768]{1,0:T(8,128)}, f32[96,3072]{1,0:T(8,128)}, /*index=5*/f32[384,768]{1,0:T(8,128)}) async-done(((f32[96,768]{1,0:T(8,128)}, f32[96,768]{1,0:T(8,128)}, f32[96,768]{1,0:T(8,128)}, f32[96,768]{1,0:T(8,128)}, f32[96,3072]{1,0:T(8,128)}, /*index=5*/f32[384,768]{1,0:T(8,128)}), ...) | async-done | bytes 3538960 | tf_op jit(solution)/shard_map/psum | solution.py:285
  (232 shorter events, 216.8 us)
Async XLA Ops:
  7.2 65.3 %all-gather.7.cloned.1.call-start = ((), (), s32[]{:S(2)}) async-start(), calls=%async_computation.6 | async-start | bytes 1327104 | tf_op jit(solution)/shard_map/all_gather | solution.py:133
  7.9 88.4 %all-gather.9.cloned.1.call-start = ((), (), s32[]{:S(2)}) async-start(), calls=%async_computation.7 | async-start | bytes 1327104 | tf_op jit(solution)/shard_map/all_gather | solution.py:131
  8.7 129.7 %all-gather.11.cloned.1.call-start = ((), (), s32[]{:S(2)}) async-start(), calls=%async_computation.8 | async-start | bytes 1327104 | tf_op jit(solution)/shard_map/all_gather | solution.py:132
  9.4 196.6 %all-gather.13.cloned.1.call-start = ((), (), s32[]{:S(2)}) async-start(), calls=%async_computation.9 | async-start | bytes 1327104 | tf_op jit(solution)/shard_map/all_gather | solution.py:134
  10.0 251.0 %all-gather.15.cloned.1.call-start = ((), (), s32[]{:S(2)}) async-start(), calls=%async_computation.10 | async-start | bytes 5308416 | tf_op jit(solution)/shard_map/all_gather | solution.py:174
  10.6 330.5 %all-gather.17.cloned.1.call-start = ((), (), s32[]{:S(2)}) async-start(), calls=%async_computation.11 | async-start | bytes 5308416 | tf_op jit(solution)/shard_map/all_gather | solution.py:176
  10.6 50.5 %collective-permute-start = (bf16[384]{0:T(512)(128)(2,1)}, bf16[384]{0:T(512)(128)(2,1)S(1)}, u32[]{:S(2)}, u32[]{:S(2)}) collective-permute-start(bf16[384]{0:T(512)(128)(2,1)} %param.32), channel_id=1, source_target_pairs={{0,7},{1,0},{2,1},{3,2},{4,3},{5,4},{6,5},{7,6},{8,15},{9,8},{10,9... | collective-permute-start | bytes 2312 | tf_op jit(solution)/shard_map/ppermute | solution.py:24
  16.7 568.2 %reduce-scatter.13.cloned.1.call-start = ((), (), s32[]{:S(2)}) async-start(), calls=%async_computation.15 | async-start | bytes 2654208 | tf_op jit(solution)/shard_map/reduce_scatter | solution.py:290
  59.8 146.2 %copy-start.34 = (f32[640]{0:T(1024)}, f32[640]{0:T(1024)S(1)}, u32[]{:S(2)}) copy-start(f32[640]{0:T(1024)S(1)} %slice_convert_fusion.8) | copy-start | bytes 7684
  59.9 281.2 %copy-start.32 = (f32[640]{0:T(1024)}, f32[640]{0:T(1024)S(1)}, u32[]{:S(2)}) copy-start(f32[640]{0:T(1024)S(1)} %get-tuple-element.92) | copy-start | bytes 7684
  61.8 3.7 collective-permute-start.1
  66.2 4.5 collective-permute-start.2
  67.1 138.9 %copy-start.25 = (pred[1600]{0:T(1024)(128)(4,1)}, pred[1600]{0:T(1024)(128)(4,1)S(1)}, u32[]{:S(2)}) copy-start(pred[1600]{0:T(1024)(128)(4,1)S(1)} %broadcast_in_dim.36) | copy-start | bytes 4804
  152.9 15.4 %copy-start.2 = (bf16[4,400,10,64]{1,0,3,2:T(4,128)(2,1)}, bf16[4,400,10,64]{1,0,3,2:T(4,128)(2,1)S(1)}, u32[]{:S(2)}) copy-start(bf16[4,400,10,64]{1,0,3,2:T(4,128)(2,1)S(1)} %reshape.146) | copy-start | bytes 6144004
  182.3 16.0 %copy-start.20 = (f32[4,10,400]{2,1,0:T(8,128)}, f32[4,10,400]{2,1,0:T(8,128)S(1)}, u32[]{:S(2)}) copy-start(f32[4,10,400]{2,1,0:T(8,128)S(1)} %fusion) | copy-start | bytes 192004
  261.0 80.1 %copy-start.36 = (f32[640]{0:T(1024)S(1)}, f32[640]{0:T(1024)}, u32[]{:S(2)}) copy-start(f32[640]{0:T(1024)} %slice_convert_fusion.2) | copy-start | bytes 7684
  363.8 21.9 %copy-start.13 = (bf16[1600,640]{1,0:T(8,128)(2,1)}, bf16[1600,640]{1,0:T(8,128)(2,1)S(1)}, u32[]{:S(2)}) copy-start(bf16[1600,640]{1,0:T(8,128)(2,1)S(1)} %get-tuple-element.60) | copy-start | bytes 6144004
  408.7 176.3 %reduce-scatter.11.cloned.1.call-start = ((), (), s32[]{:S(2)}) async-start(), calls=%async_computation.14 | async-start | bytes 2654208 | tf_op jit(solution)/shard_map/reduce_scatter | solution.py:289
  456.4 162.6 %reduce-scatter.9.cloned.1.call-start = ((), (), s32[]{:S(2)}) async-start(), calls=%async_computation.13 | async-start | bytes 2654208 | tf_op jit(solution)/shard_map/reduce_scatter | solution.py:288
  481.9 28.1 %copy-start.4 = (bf16[4,400,10,64]{1,0,3,2:T(4,128)(2,1)S(1)}, bf16[4,400,10,64]{1,0,3,2:T(4,128)(2,1)}, u32[]{:S(2)}) copy-start(bf16[4,400,10,64]{1,0,3,2:T(4,128)(2,1)} %reshape.145) | copy-start | bytes 6144004
  530.4 160.0 %reduce-scatter.7.cloned.1.call-start = ((), (), s32[]{:S(2)}) async-start(), calls=%async_computation.12 | async-start | bytes 2654208 | tf_op jit(solution)/shard_map/reduce_scatter | solution.py:287
  552.2 304.3 %reduce-scatter.15.cloned.1.call-start = ((), (), s32[]{:S(2)}) async-start(), calls=%async_computation.16 | async-start | bytes 10616832 | tf_op jit(solution)/shard_map/reduce_scatter | solution.py:297
  567.7 454.7 %reduce-scatter.17.cloned.1.call-start = ((), (), s32[]{:S(2)}) async-start(), calls=%async_computation.17 | async-start | bytes 10616832 | tf_op jit(solution)/shard_map/reduce_scatter | solution.py:299
  583.5 516.9 %all-reduce.41.cloned.1.call-start = ((), (), s32[]{:S(2)}) async-start(), calls=%async_computation.18 | async-start | bytes 7077888 | tf_op jit(solution)/shard_map/psum | solution.py:285
  (29 other events, 163.0 us)
Sparse Core Ops, SparseCore 0:
  10.2 43.9 all-gather.6
  56.4 39.8 all-gather.8
  98.5 39.8 all-gather.10
  140.4 39.8 all-gather.12
  182.3 78.6 all-gather.14
  263.0 78.0 all-gather.16
  408.8 67.1 reduce-scatter.12
  479.5 68.0 reduce-scatter.10
  551.0 67.9 reduce-scatter.8
  622.4 67.9 reduce-scatter.6
  694.0 162.4 reduce-scatter.14
  860.0 162.3 reduce-scatter.16
  1025.2 75.1 all-reduce.40
